TPU v7x, 32 devices: a whole 2x2x4 slice. The times are simulated.
32 devices in a mesh: replica: 4 (over x, core), shard: 8 (over z, y).
Axes of the slice: x: 2, y: 2, z: 4, core: 2. Of those that a mesh axis runs over, the one named last changes fastest.
Arguments:
- tokens: bfloat16 [32768, 768], P(('replica', 'shard')), may hold values from -6 to 6
- gain_attn: bfloat16 [768], P('shard'), may hold values from 0.099609375 to 1.8984375
- w_qkv: bfloat16 [768, 2304], P('shard'), may hold values from -0.3125 to 0.3125
- w_out: bfloat16 [768, 768], P('shard'), may hold values from -0.875 to 0.875
- gain_ffn: bfloat16 [768], P('shard'), may hold values from 0.099609375 to 1.8984375
- w_in: bfloat16 [768, 2304], P('shard'), may hold values from -0.21875 to 0.21875
- w_down: bfloat16 [1152, 768], P('shard'), may hold values from -0.1875 to 0.1875
- cotangent: bfloat16 [32768, 768], P(('replica', 'shard')), may hold values from -6 to 6
Outputs:
- output: bfloat16 [32768, 768], P(('replica', 'shard'))
- input_grad: bfloat16 [32768, 768], P(('replica', 'shard'))
- grad_gain_attn: float32 [768], P('shard')
- grad_qkv: float32 [768, 2304], P('shard')
- grad_out: float32 [768, 768], P('shard')
- grad_gain_ffn: float32 [768], P('shard')
- grad_in: float32 [768, 2304], P('shard')
- grad_down: float32 [1152, 768], P('shard')
All inputs are finite; a program needn't handle non-finite values.
Results may differ from a plain program's by a relative error of at most 0.018.
Values may be sent and summed in bfloat16 or wider, within the bound.
A program may use at most 128 MiB of HBM per device.

v0:
```python
import math
import jax
import jax.numpy as jnp
from jax import lax
from jax.sharding import PartitionSpec as P

D = 768
HEADS = 12
HEAD_DIM = 64
FF = 1152
WINDOW = 128
LENGTH = 1024
epsilon = 1e-05


def normalize(values):
    centre = values - jnp.mean(values, axis=-1, keepdims=True)
    inverse = lax.rsqrt(jnp.mean(centre * centre, axis=-1, keepdims=True) + epsilon)
    return (centre * inverse, inverse)


def norm_back(grad_norm, standard, inverse, gain):
    scaled = grad_norm * gain
    return inverse * (
        scaled
        - jnp.mean(scaled, axis=-1, keepdims=True)
        - standard * jnp.mean(scaled * standard, axis=-1, keepdims=True)
    )


def rotary_tables(count):
    half_dim = HEAD_DIM // 2
    freqs = 10000.0 ** (-(jnp.arange(half_dim, dtype=jnp.float32) * 2.0) / HEAD_DIM)
    places = (jnp.arange(count, dtype=jnp.int32) % LENGTH).astype(jnp.float32)
    angles = places[:, None] * freqs[None, :]
    angles = jnp.concatenate([angles, angles], axis=1)
    return (jnp.cos(angles)[:, None, :], jnp.sin(angles)[:, None, :])


def rotate_half(values):
    half_dim = values.shape[-1] // 2
    return jnp.concatenate([-values[..., half_dim:], values[..., :half_dim]], axis=-1)


def rotate_back(values):
    half_dim = values.shape[-1] // 2
    return jnp.concatenate([values[..., half_dim:], -values[..., :half_dim]], axis=-1)


def windows(field, block_rows, margin):
    seq_count = field.shape[0] // LENGTH
    blocks = LENGTH // block_rows
    shaped = field.reshape(seq_count, LENGTH, HEADS, HEAD_DIM)
    padded = jnp.pad(shaped, ((0, 0), (margin, block_rows - margin), (0, 0), (0, 0)))
    first = padded[:, :LENGTH].reshape(seq_count, blocks, block_rows, HEADS, HEAD_DIM)
    second = padded[:, block_rows : block_rows + LENGTH].reshape(
        seq_count, blocks, block_rows, HEADS, HEAD_DIM
    )
    joined = jnp.concatenate([first, second[:, :, : 2 * margin]], axis=2)
    return joined.reshape(seq_count * blocks, block_rows + 2 * margin, HEADS, HEAD_DIM)


def unwindow(field, block_rows, margin):
    blocks = LENGTH // block_rows
    seq_count = field.shape[0] // blocks
    shaped = field.reshape(seq_count, blocks, block_rows + 2 * margin, HEADS, HEAD_DIM)
    first = shaped[:, :, :block_rows].reshape(seq_count, LENGTH, HEADS, HEAD_DIM)
    second = jnp.pad(
        shaped[:, :, block_rows:], ((0, 0), (0, 0), (0, block_rows - 2 * margin), (0, 0), (0, 0))
    )
    second = second.reshape(seq_count, LENGTH, HEADS, HEAD_DIM)
    whole = jnp.pad(first, ((0, 0), (0, block_rows), (0, 0), (0, 0))) + jnp.pad(
        second, ((0, 0), (block_rows, 0), (0, 0), (0, 0))
    )
    return whole[:, margin : margin + LENGTH].reshape(seq_count * LENGTH, HEADS, HEAD_DIM)


def to_items(field):
    per_group = math.gcd(HEADS, 4)
    head_groups = HEADS // per_group
    count, rows = (field.shape[0], field.shape[1])
    shaped = field.reshape(count, rows, head_groups, per_group, HEAD_DIM).transpose(0, 2, 1, 3, 4)
    return shaped.reshape(count * head_groups, rows, per_group, HEAD_DIM)


def from_items(field):
    per_group = math.gcd(HEADS, 4)
    head_groups = HEADS // per_group
    count, rows = (field.shape[0] // head_groups, field.shape[1])
    shaped = field.reshape(count, head_groups, rows, per_group, HEAD_DIM).transpose(0, 2, 1, 3, 4)
    return shaped.reshape(count, rows, HEADS, HEAD_DIM)


def block_scores(query_part, key_part, start, block_rows, margin):
    span = key_part.shape[0]
    query_pos = start + jnp.arange(block_rows, dtype=jnp.int32)[:, None]
    key_pos = start - margin + jnp.arange(span, dtype=jnp.int32)[None, :]
    allowed = (key_pos >= 0) & (key_pos < LENGTH) & (jnp.abs(query_pos - key_pos) <= margin)
    raw = jnp.einsum(
        "qhd,khd->hqk", query_part, key_part, preferred_element_type=jnp.float32
    ) * HEAD_DIM ** (-0.5)
    return jnp.where(allowed[None], raw, -1e30)


def block_starts(count, block_rows):
    per_group = math.gcd(HEADS, 4)
    blocks = LENGTH // block_rows
    starts = jnp.arange(count, dtype=jnp.int32) % blocks * block_rows
    return jnp.repeat(starts, HEADS // per_group)


def attend_forward(queries, keys, values):
    count_tok = queries.shape[0]
    block_rows = min(512, LENGTH)
    margin = WINDOW // 2
    query_items = to_items(queries.reshape(count_tok // block_rows, block_rows, HEADS, HEAD_DIM))
    key_items = to_items(windows(keys, block_rows, margin))
    value_items = to_items(windows(values, block_rows, margin))
    starts = block_starts(count_tok // block_rows, block_rows)

    def one_block(pieces):
        query_part, key_part, value_part, start = pieces
        scores = block_scores(query_part, key_part, start, block_rows, margin)
        top = jnp.max(scores, axis=-1, keepdims=True)
        expo = jnp.exp(scores - top)
        total = jnp.sum(expo, axis=-1, keepdims=True)
        probs = (expo / total).astype(jnp.bfloat16)
        mixed = jnp.einsum("hqk,khd->qhd", probs, value_part, preferred_element_type=jnp.float32)
        return (mixed.astype(jnp.bfloat16), top[..., 0] + jnp.log(total[..., 0]))

    mixed, log_totals = lax.map(one_block, (query_items, key_items, value_items, starts))
    return (from_items(mixed).reshape(count_tok, D), log_totals)


def attend_backward(queries, keys, values, grad_mixed, log_totals):
    count_tok = queries.shape[0]
    block_rows = min(512, LENGTH)
    margin = WINDOW // 2
    scale = HEAD_DIM ** (-0.5)
    query_items = to_items(queries.reshape(count_tok // block_rows, block_rows, HEADS, HEAD_DIM))
    grad_items = to_items(grad_mixed.reshape(count_tok // block_rows, block_rows, HEADS, HEAD_DIM))
    key_items = to_items(windows(keys, block_rows, margin))
    value_items = to_items(windows(values, block_rows, margin))
    starts = block_starts(count_tok // block_rows, block_rows)

    def one_block(pieces):
        query_part, key_part, value_part, grad_part, log_part, start = pieces
        scores = block_scores(query_part, key_part, start, block_rows, margin)
        probs = jnp.exp(scores - log_part[..., None])
        grad_probs = jnp.einsum(
            "qhd,khd->hqk", grad_part, value_part, preferred_element_type=jnp.float32
        )
        centre = jnp.sum(grad_probs * probs, axis=-1, keepdims=True)
        grad_scores = (probs * (grad_probs - centre)).astype(jnp.bfloat16)
        grad_query = (
            jnp.einsum("hqk,khd->qhd", grad_scores, key_part, preferred_element_type=jnp.float32)
            * scale
        )
        grad_key = (
            jnp.einsum("hqk,qhd->khd", grad_scores, query_part, preferred_element_type=jnp.float32)
            * scale
        )
        grad_value = jnp.einsum(
            "hqk,qhd->khd",
            probs.astype(jnp.bfloat16),
            grad_part,
            preferred_element_type=jnp.float32,
        )
        return (grad_query, grad_key, grad_value)

    grad_query, grad_key, grad_value = lax.map(
        one_block, (query_items, key_items, value_items, grad_items, log_totals, starts)
    )
    grad_query = from_items(grad_query).reshape(count_tok, HEADS, HEAD_DIM)
    grad_key = unwindow(from_items(grad_key), block_rows, margin)
    grad_value = unwindow(from_items(grad_value), block_rows, margin)
    return (grad_query, grad_key, grad_value)


def body(tokens, gain_attn, w_qkv, w_out, gain_ffn, w_in, w_down, cotangent):
    count_tok = tokens.shape[0]
    gain_one, joint_weight, out_weight = (
        lax.all_gather(gain_attn, "shard", axis=0, tiled=True),
        lax.all_gather(w_qkv, "shard", axis=0, tiled=True),
        lax.all_gather(w_out, "shard", axis=0, tiled=True),
    )
    gain_two, in_weight, down_weight = (
        lax.all_gather(gain_ffn, "shard", axis=0, tiled=True),
        lax.all_gather(w_in, "shard", axis=0, tiled=True),
        lax.all_gather(w_down, "shard", axis=0, tiled=True),
    )
    stream = tokens.astype(jnp.float32)
    standard_one, inverse_one = normalize(stream)
    normed_attn = (standard_one * gain_one.astype(jnp.float32)).astype(jnp.bfloat16)
    projected = jnp.dot(normed_attn, joint_weight, preferred_element_type=jnp.float32)
    projected = projected.reshape(count_tok, 3, HEADS, HEAD_DIM)
    cosine, sine = rotary_tables(count_tok)
    raw_query = projected[:, 0]
    raw_key = projected[:, 1]
    queries = (raw_query * cosine + rotate_half(raw_query) * sine).astype(jnp.bfloat16)
    keys = (raw_key * cosine + rotate_half(raw_key) * sine).astype(jnp.bfloat16)
    values = projected[:, 2].astype(jnp.bfloat16)
    attended, log_totals = attend_forward(queries, keys, values)
    after_attn = stream + jnp.dot(attended, out_weight, preferred_element_type=jnp.float32)
    standard_two, inverse_two = normalize(after_attn)
    normed_ffn = (standard_two * gain_two.astype(jnp.float32)).astype(jnp.bfloat16)
    gate_up = jnp.dot(normed_ffn, in_weight, preferred_element_type=jnp.float32)
    lifted = gate_up[:, :FF]
    gate_part = gate_up[:, FF:]
    normal_cdf = 0.5 * (1.0 + lax.erf(lifted * 0.7071067811865476))
    gelu_value = lifted * normal_cdf
    activated = (gelu_value * gate_part).astype(jnp.bfloat16)
    final = after_attn + jnp.dot(activated, down_weight, preferred_element_type=jnp.float32)
    output = final.astype(jnp.bfloat16)
    gain_one, joint_weight, out_weight = (
        lax.all_gather(gain_attn, "shard", axis=0, tiled=True),
        lax.all_gather(w_qkv, "shard", axis=0, tiled=True),
        lax.all_gather(w_out, "shard", axis=0, tiled=True),
    )
    gain_two, in_weight, down_weight = (
        lax.all_gather(gain_ffn, "shard", axis=0, tiled=True),
        lax.all_gather(w_in, "shard", axis=0, tiled=True),
        lax.all_gather(w_down, "shard", axis=0, tiled=True),
    )
    grad_final = cotangent.astype(jnp.float32)
    grad_down = jnp.einsum("tf,td->fd", activated, cotangent, preferred_element_type=jnp.float32)
    grad_act = jnp.einsum("td,fd->tf", cotangent, down_weight, preferred_element_type=jnp.float32)
    density = jnp.exp(-0.5 * lifted * lifted) * 0.3989422804014327
    grad_lifted = grad_act * gate_part * (normal_cdf + lifted * density)
    grad_gate = grad_act * gelu_value
    grad_gate_up = jnp.concatenate([grad_lifted, grad_gate], axis=1).astype(jnp.bfloat16)
    grad_in = jnp.einsum("td,te->de", normed_ffn, grad_gate_up, preferred_element_type=jnp.float32)
    grad_norm_ffn = jnp.einsum(
        "te,de->td", grad_gate_up, in_weight, preferred_element_type=jnp.float32
    )
    grad_gain_ffn = jnp.sum(grad_norm_ffn * standard_two, axis=0)
    grad_after = grad_final + norm_back(
        grad_norm_ffn, standard_two, inverse_two, gain_two.astype(jnp.float32)
    )
    ffn_members = (grad_gain_ffn, grad_in, grad_down)
    owned_gain_ffn, owned_in, owned_down = (
        lax.psum_scatter(ffn_members[0], "shard", scatter_dimension=0, tiled=True),
        lax.psum_scatter(ffn_members[1], "shard", scatter_dimension=0, tiled=True),
        lax.psum_scatter(ffn_members[2], "shard", scatter_dimension=0, tiled=True),
    )
    grad_branch = grad_after.astype(jnp.bfloat16)
    grad_out = jnp.einsum("td,te->de", attended, grad_branch, preferred_element_type=jnp.float32)
    grad_attended = jnp.einsum(
        "te,de->td", grad_branch, out_weight, preferred_element_type=jnp.float32
    ).astype(jnp.bfloat16)
    grad_query, grad_key, grad_value = attend_backward(
        queries, keys, values, grad_attended, log_totals
    )
    grad_query = grad_query * cosine + rotate_back(grad_query * sine)
    grad_key = grad_key * cosine + rotate_back(grad_key * sine)
    grad_projected = jnp.stack([grad_query, grad_key, grad_value], axis=1)
    grad_projected = grad_projected.reshape(count_tok, 3 * D).astype(jnp.bfloat16)
    grad_qkv = jnp.einsum(
        "td,te->de", normed_attn, grad_projected, preferred_element_type=jnp.float32
    )
    grad_norm_attn = jnp.einsum(
        "te,de->td", grad_projected, joint_weight, preferred_element_type=jnp.float32
    )
    grad_gain_attn = jnp.sum(grad_norm_attn * standard_one, axis=0)
    input_grad = grad_after + norm_back(
        grad_norm_attn, standard_one, inverse_one, gain_one.astype(jnp.float32)
    )
    attn_members = (grad_gain_attn, grad_qkv, grad_out)
    owned_gain_attn, owned_qkv, owned_out = (
        lax.psum_scatter(attn_members[0], "shard", scatter_dimension=0, tiled=True),
        lax.psum_scatter(attn_members[1], "shard", scatter_dimension=0, tiled=True),
        lax.psum_scatter(attn_members[2], "shard", scatter_dimension=0, tiled=True),
    )
    summed = (
        lax.psum(owned_gain_attn.astype(jnp.bfloat16), "replica").astype(jnp.float32),
        lax.psum(owned_qkv.astype(jnp.bfloat16), "replica").astype(jnp.float32),
        lax.psum(owned_out.astype(jnp.bfloat16), "replica").astype(jnp.float32),
        lax.psum(owned_gain_ffn.astype(jnp.bfloat16), "replica").astype(jnp.float32),
        lax.psum(owned_in.astype(jnp.bfloat16), "replica").astype(jnp.float32),
        lax.psum(owned_down.astype(jnp.bfloat16), "replica").astype(jnp.float32),
    )
    return (
        output,
        input_grad.astype(jnp.bfloat16),
        summed[0],
        summed[1],
        summed[2],
        summed[3],
        summed[4],
        summed[5],
    )


def solution(mesh):
    return jax.shard_map(
        body,
        mesh=mesh,
        in_specs=(
            P(("replica", "shard"), None),
            P("shard"),
            P("shard", None),
            P("shard", None),
            P("shard"),
            P("shard", None),
            P("shard", None),
            P(("replica", "shard"), None),
        ),
        out_specs=(
            P(("replica", "shard"), None),
            P(("replica", "shard"), None),
            P("shard"),
            P("shard", None),
            P("shard", None),
            P("shard"),
            P("shard", None),
            P("shard", None),
        ),
        check_vma=False,
    )
```

profile of v0, /device:TPU:0, one launch (start us, length us, event | category | flops | bytes accessed | tf_op | source)
XLA Modules:
  0.0 722.2 jit_solution(9472683614992483625)
XLA Ops:
  14.4 23.5 %all-reduce.13 = (bf16[768]{0:T(1024)(128)(2,1)S(1)}, bf16[768]{0:T(1024)(128)(2,1)S(1)}) all-reduce(bf16[768]{0:T(1024)(128)(2,1)S(1)} %dynamic-update-slice, bf16[768]{0:T(1024)(128)(2,1)S(1)} %dynamic-update-slice.1), channel_id=1, replica_groups=mesh['replica'=4,'shard'=8] {'shard'}, use_global_device_ids=true, to_apply=%add.8 | all-reduce | flops 1536 | bytes 6144
  46.5 31.9 %all-gather.5.cloned.1.call-done = bf16[768,2304]{1,0:T(8,128)(2,1)} async-done(((bf16[96,2304]{1,0:T(8,128)(2,1)}), bf16[768,2304]{1,0:T(8,128)(2,1)}) %all-gather.5.cloned.1.call-update) | async-done | bytes 3538960 | tf_op jit(solution)/shard_map/all_gather | solution.py:184
  78.4 6.0 fusion.96
  112.8 5.6 squeeze.70
  143.6 61.0 %while.30 = (s32[]{:T(128)}, bf16[6,512,4,64]{1,3,2,0:T(8,128)(2,1)}, f32[6,4,512]{2,1,0:T(4,128)}, bf16[6,640,4,64]{1,3,2,0:T(8,128)(2,1)}, s32[6]{0:T(128)S(1)...) while((s32[]{:T(128)}, ...), condition=%wide.region_5.6_spmd, body=%wide.region_2.5_spmd.sunk | while | flops 352716416 | bytes 18297728 | solution.py:131
  214.7 10.7 %fusion.110 = f32[1024,2304]{1,0:T(8,128)} fusion(bf16[768,2304]{1,0:T(8,128)(2,1)} %all-gather.9.cloned.1.call-done, f32[1024,768]{0,1:T(8,128)} %copy-done.4, f32[768]{0:T(1024)S(1)} %convert_element_type.164, f32[1024]{0:T(1024)S(1)} %add_rsqrt_fusion, f32[1024]{0:T(1024)S(1)} %broadcast_multiply_fusion.7), kind=kOutput, calls=%fused_computation.187 | convolution fusion | flops 3627024384 | bytes 16133120 | tf_op jit(solution)/shard_map/dot_general | solution.py:207
  225.4 7.5 %all-gather.11.cloned.1.call-done = bf16[1152,768]{1,0:T(8,128)(2,1)} async-done(((bf16[144,768]{1,0:T(8,128)(2,1)}), bf16[1152,768]{1,0:T(8,128)(2,1)}) %all-gather.11.cloned.1.call-update) | async-done | bytes 1769488 | tf_op jit(solution)/shard_map/all_gather | solution.py:190
  232.8 9.2 %fusion.61 = (bf16[1024,1152]{1,0:T(8,128)(2,1)S(1)}, bf16[1024,1152]{1,0:T(8,128)(2,1)S(1)}, bf16[1024,1152]{1,0:T(8,128)(2,1)}) fusion(f32[1024,2304]{1,0:T(8,128)} %fusion.110, bf16[1024,768]{1,0:T(8,128)(2,1)S(1)} %copy-done.20, bf16[1152,768]{1,0:T(8,128)(2,1)} %all-gather.11.cloned.1.call-done), kind=kOutput, calls=%fused_computation.78 | convolution fusion | flops 1830813696 | bytes 19857408 | tf_op jit(solution)/shard_map/td,fd->tf/dot_general | solution.py:227
  252.6 5.5 fusion.113
  270.5 9.3 %fusion.83 = f32[768,2304]{1,0:T(8,128)} fusion(bf16[1024,1152]{1,0:T(8,128)(2,1)} %copy-done.36, bf16[1024,1152]{1,0:T(8,128)(2,1)} %copy-done.35, f32[1024,768]{0,1:T(8,128)S(1)} %copy-done.6, f32[768]{0:T(1024)S(1)} %convert_element_type.164, f32[1024]{0:T(1024)S(1)} %add_rsqrt_fusion, f32[1024]{0:T(1024)S(1)} %broadcast_multiply_fusion.7), kind=kOutput, calls=%fused_computation.123 | convolution fusion | flops 3636461568 | bytes 14953472 | tf_op jit(solution)/shard_map/td,te->de/dot_general | solution.py:232
  279.8 95.7 %while.31 = (s32[]{:T(128)}, f32[6,512,4,64]{1,3,2,0:T(8,128)}, f32[6,640,4,64]{1,3,2,0:T(8,128)}, f32[6,640,4,64]{1,3,2,0:T(8,128)}, bf16[6,640,4,64]{1,3,2,0:T...) while((s32[]{:T(128)}, f32[6,512,4,64]{1,3,2,0:T(8,128)}, ...), condition=%wide.region_12.13_spmd, body=%wide.region_10.12_spmd.sunk | while | flops 860128896 | bytes 44572060 | solution.py:171
  375.6 5.2 copy.70
  394.9 5.2 copy.71
  411.2 5.6 reshape.526
  420.8 5.6 reshape.532
  426.4 6.0 reshape.531
  445.9 6.2 fusion.94
  452.8 9.3 %fusion.74 = (f32[768]{0:T(1024)S(1)}, f32[1024]{0:T(1024)S(1)}, f32[1024]{0:T(1024)S(1)}, f32[1024,768]{0,1:T(8,128)}) fusion(bf16[1024,768]{0,1:T(8,128)(2,1)S(1)} %copy-done.2, f32[1024]{0:T(1024)S(1)} %copy-done.26, f32[1024]{0:T(1024)S(1)} %copy-done.24, f32[768]{0:T(1024)S(1)} %copy-done.28, bf16[768,2304]{1,0:T(8,128)(2,1)} %all-gather.5.cloned.1.call-done, ...), kind=kOutput, calls=%fused_computation.97 | convolution fusion | flops 3630953728 | bytes 12998656 | tf_op jit(solution)/shard_map/te,de->td/dot_general | solution.py:261
  462.1 20.3 %all-reduce.12 = (bf16[768]{0:T(1024)(128)(2,1)S(1)}, bf16[768]{0:T(1024)(128)(2,1)S(1)}) all-reduce(f32[768]{0:T(1024)S(1)} %get-tuple-element.264, f32[768]{0:T(1024)S(1)} %copy-done.29), channel_id=2, replica_groups=mesh['replica'=4,'shard'=8] {'shard'}, use_global_device_ids=true, to_apply=%region_16.17.clone | all-reduce | flops 1536 | bytes 9216
  482.6 6.2 all-reduce.14
  498.8 36.7 %reduce-scatter.9.cloned.1.call-done = f32[96,2304]{1,0:T(8,128)} async-done(((f32[768,2304]{1,0:T(8,128)}), f32[96,2304]{1,0:T(8,128)}) %reduce-scatter.9.cloned.1.call-update) | async-done | bytes 884752 | tf_op jit(solution)/shard_map/reduce_scatter | solution.py:243
  537.5 130.3 %reduce-scatter.5.cloned.1.call-done = f32[96,2304]{1,0:T(8,128)} async-done(((f32[768,2304]{1,0:T(8,128)}), f32[96,2304]{1,0:T(8,128)}) %reduce-scatter.5.cloned.1.call-update) | async-done | bytes 884752 | tf_op jit(solution)/shard_map/reduce_scatter | solution.py:271
  669.8 5.6 add_convert_fusion
  678.0 31.1 %all-reduce.18.cloned.1.call-done = (bf16[96,2304]{1,0:T(8,128)(2,1)}, bf16[96,768]{1,0:T(8,128)(2,1)}, bf16[96,2304]{1,0:T(8,128)(2,1)}, bf16[144,768]{1,0:T(8,128)(2,1)}) async-done(((bf16[96,2304]{1,0:T(8,128)(2,1)}, bf16[96,768]{1,0:T(8,128)(2,1)}, bf16[96,2304]{1,0:T(8,128)(2,1)}, bf16[144,768]{1,0:T(8,128)(2,1)}), (bf16[96,2304]{1,0:T(8,128)(2,1)}, bf16[96,768]{1,0:T(8,128)(2,1)}, ...) | async-done | bytes 1253392 | tf_op jit(solution)/shard_map/psum | solution.py:276
  (319 shorter events, 315.2 us)
Async XLA Ops:
  7.2 71.2 %all-gather.5.cloned.1.call-start = ((), (), s32[]{:S(2)}) async-start(), calls=%async_computation.4 | async-start | bytes 3981312 | tf_op jit(solution)/shard_map/all_gather | solution.py:184
  7.9 201.3 %all-gather.7.cloned.1.call-start = ((), (), s32[]{:S(2)}) async-start(), calls=%async_computation.5 | async-start | bytes 1327104 | tf_op jit(solution)/shard_map/all_gather | solution.py:185
  8.6 206.0 %all-gather.9.cloned.1.call-start = ((), (), s32[]{:S(2)}) async-start(), calls=%async_computation.6 | async-start | bytes 3981312 | tf_op jit(solution)/shard_map/all_gather | solution.py:189
  9.4 223.4 %all-gather.11.cloned.1.call-start = ((), (), s32[]{:S(2)}) async-start(), calls=%async_computation.7 | async-start | bytes 1990656 | tf_op jit(solution)/shard_map/all_gather | solution.py:190
  10.0 485.3 %reduce-scatter.7.cloned.1.call-start = ((), (), s32[]{:S(2)}) async-start(), calls=%async_computation.9 | async-start | bytes 2654208 | tf_op jit(solution)/shard_map/reduce_scatter | solution.py:272
  11.9 197.4 %copy-start.1 = (bf16[1024,768]{0,1:T(8,128)(2,1)}, bf16[1024,768]{0,1:T(8,128)(2,1)S(1)}, u32[]{:S(2)}) copy-start(bf16[1024,768]{0,1:T(8,128)(2,1)S(1)} %copy.59) | copy-start | bytes 4718596
  12.1 66.2 %copy-start.23 = (f32[1024]{0:T(1024)}, f32[1024]{0:T(1024)S(1)}, u32[]{:S(2)}) copy-start(f32[1024]{0:T(1024)S(1)} %broadcast_multiply_fusion.8) | copy-start | bytes 12292
  12.6 71.7 %copy-start.25 = (f32[1024]{0:T(1024)}, f32[1024]{0:T(1024)S(1)}, u32[]{:S(2)}) copy-start(f32[1024]{0:T(1024)S(1)} %add_rsqrt_fusion.1) | copy-start | bytes 12292
  37.9 46.5 %copy-start.27 = (f32[768]{0:T(1024)}, f32[768]{0:T(1024)S(1)}, u32[]{:S(2)}) copy-start(f32[768]{0:T(1024)S(1)} %convert_element_type.157) | copy-start | bytes 9220
  39.0 51.3 %copy-start.16 = (f32[1024,64]{0,1:T(8,128)}, f32[1024,64]{0,1:T(8,128)S(1)}, u32[]{:S(2)}) copy-start(f32[1024,64]{0,1:T(8,128)S(1)} %get-tuple-element.338) | copy-start | bytes 786436
  39.0 51.3 %copy-start.18 = (f32[1024,64]{0,1:T(8,128)}, f32[1024,64]{0,1:T(8,128)S(1)}, u32[]{:S(2)}) copy-start(f32[1024,64]{0,1:T(8,128)S(1)} %get-tuple-element.339) | copy-start | bytes 786436
  214.7 18.2 %copy-start.20 = (bf16[1024,768]{1,0:T(8,128)(2,1)S(1)}, bf16[1024,768]{1,0:T(8,128)(2,1)}, u32[]{:S(2)}) copy-start(bf16[1024,768]{1,0:T(8,128)(2,1)} %param.19) | copy-start | bytes 4718596
  232.8 9.2 %copy-start.5 = (f32[1024,768]{0,1:T(8,128)S(1)}, f32[1024,768]{0,1:T(8,128)}, u32[]{:S(2)}) copy-start(f32[1024,768]{0,1:T(8,128)} %copy-done.4) | copy-start | bytes 9437188
  232.8 9.2 %copy-start.31 = (bf16[768,2304]{1,0:T(8,128)(2,1)S(1)}, bf16[768,2304]{1,0:T(8,128)(2,1)}, u32[]{:S(2)}) copy-start(bf16[768,2304]{1,0:T(8,128)(2,1)} %all-gather.9.cloned.1.call-done) | copy-start | bytes 10616836
  242.0 4.9 copy-start.35
  242.0 4.9 copy-start.36
  242.1 4.9 copy-start.11
  252.6 244.5 %reduce-scatter.11.cloned.1.call-start = ((), (), s32[]{:S(2)}) async-start(), calls=%async_computation.11 | async-start | bytes 3981312 | tf_op jit(solution)/shard_map/reduce_scatter | solution.py:244
  258.1 277.4 %reduce-scatter.9.cloned.1.call-start = ((), (), s32[]{:S(2)}) async-start(), calls=%async_computation.10 | async-start | bytes 7962624 | tf_op jit(solution)/shard_map/reduce_scatter | solution.py:243
  279.8 388.0 %reduce-scatter.5.cloned.1.call-start = ((), (), s32[]{:S(2)}) async-start(), calls=%async_computation.8 | async-start | bytes 7962624 | tf_op jit(solution)/shard_map/reduce_scatter | solution.py:271
  452.2 256.9 %all-reduce.18.cloned.1.call-start = ((), (), s32[]{:S(2)}) async-start(), calls=%async_computation.12 | async-start | bytes 2506752 | tf_op jit(solution)/shard_map/psum | solution.py:276
  452.8 9.3 %copy-start.29 = (f32[768]{0:T(1024)S(1)}, f32[768]{0:T(1024)}, u32[]{:S(2)}) copy-start(f32[768]{0:T(1024)} %get-tuple-element.262) | copy-start | bytes 9220
  495.3 174.5 %copy-start.7 = (f32[1024,768]{0,1:T(8,128)S(1)}, f32[1024,768]{0,1:T(8,128)}, u32[]{:S(2)}) copy-start(f32[1024,768]{0,1:T(8,128)} %copy-done.4) | copy-start | bytes 9437188
  709.0 5.7 copy-start.22
  (23 other events, 64.5 us)
Sparse Core Ops, SparseCore 0:
  10.2 68.1 all-gather.4
  80.5 39.5 all-gather.6
  122.3 63.9 all-gather.8
  188.3 44.4 all-gather.10
  252.7 68.0 reduce-scatter.6
  324.2 78.1 reduce-scatter.10
  406.1 129.3 reduce-scatter.8
  539.6 128.0 reduce-scatter.4
  671.0 38.0 all-reduce.17
where the time goes:
time: 734 us; the launch traced here: 722 us
  waiting for transfers between devices  240 us (33%)
  matrix products  179 us (24%)
  local copies, waits for them, and re-layouts  142 us (19%)
  other arithmetic  86 us (12%)
  blocking collectives  50 us (7%)
  between operations  16 us (2%)
  loops' own time  8.62 us (1%)
    reduce_scatter x1, waiting for transfers between devices, body(): lax.psum_scatter(attn_members[1], 'shard', scatter_dimension=0, tiled=True)  130 us
    unnamed x2, blocking collectives  43.8 us
    reduce_scatter x1, waiting for transfers between devices, body(): lax.psum_scatter(ffn_members[1], 'shard', scatter_dimension=0, tiled=True)  36.7 us
    all_gather x1, waiting for transfers between devices, body(): lax.all_gather(w_qkv, 'shard', axis=0, tiled=True)  31.9 us
    psum x1, waiting for transfers between devices, body(): lax.psum(owned_qkv.astype(jnp.bfloat16), 'replica').astype(jnp.float32)  31.1 us
    dot_general x12, matrix products, block_scores(): jnp.einsum('qhd,khd->hqk', query_part, key_part, preferred_element_type=j...  24.6 us
    unnamed x86, local copies, waits for them, and re-layouts  21.1 us
    dot_general x6, matrix products, one_block(): jnp.einsum('hqk,khd->qhd', probs, value_part, preferred_element_type=jnp....  20.8 us
  transfers between devices with their start and end apart: 9, of which 5 were waited for; matrix products, arithmetic and copies ran while one was open for 51% of the time, Pallas kernels for 0%

commit v1 on v0

--- a/solution.py
+++ b/solution.py
@@ -11,6 +11,19 @@
 WINDOW = 128
 LENGTH = 1024
 epsilon = 1e-05
+
+
+def collect(shard, axis, dim):
+    ways = lax.axis_size(axis)
+    up = [(d, (d + 1) % ways) for d in range(ways)]
+    down = [(d, (d - 1) % ways) for d in range(ways)]
+    earlier, later = ([shard], [shard])
+    for _ in range(ways // 2):
+        earlier.append(lax.ppermute(earlier[-1], axis, up))
+    for _ in range((ways - 1) // 2):
+        later.append(lax.ppermute(later[-1], axis, down))
+    line = jnp.concatenate([*earlier[::-1], *later[1:]], axis=dim)
+    return jnp.roll(line, (lax.axis_index(axis) - ways // 2) * shard.shape[dim], axis=dim)
 
 
 def normalize(values):
@@ -181,7 +194,7 @@
     count_tok = tokens.shape[0]
     gain_one, joint_weight, out_weight = (
         lax.all_gather(gain_attn, "shard", axis=0, tiled=True),
-        lax.all_gather(w_qkv, "shard", axis=0, tiled=True),
+        collect(w_qkv, "shard", 0),
         lax.all_gather(w_out, "shard", axis=0, tiled=True),
     )
     gain_two, in_weight, down_weight = (

time: 734 us -> 757 us (1.031)
  starting transfers between devices: 0.36 us -> 16.6 us
  waiting for transfers between devices: 240 us -> 248 us
    ppermute x0 -> x7, waiting for transfers between devices: none -> 46.6 us  [the longest x4 24.6 us: collect(): earlier.append(lax.ppermute(earlier[-1], axis, up))]
    all_gather x1, waiting for transfers between devices: 31.9 us -> 0.02 us  [body(): lax.all_gather(w_qkv, 'shard', axis=0, tiled=True)]
    ppermute x0 -> x7, starting transfers between devices: none -> 16.3 us  [the longest x3 10 us: collect(): later.append(lax.ppermute(later[-1], axis, down))]
    unnamed x86 -> x103, local copies, waits for them, and re-layouts: 21.1 us -> 23.3 us
  transfers between devices with their start and end apart: 9 -> 16, of which waited for: 5 -> 7; matrix products, arithmetic and copies ran while one was open for 51% -> 52% of each run, Pallas kernels for 0% -> 0%
where the time goes in v1:
time: 757 us; the launch traced here: 750 us
  waiting for transfers between devices  248 us (33%)
  matrix products  178 us (24%)
  local copies, waits for them, and re-layouts  144 us (19%)
  other arithmetic  85.9 us (11%)
  blocking collectives  53.2 us (7%)
  starting transfers between devices  16.6 us (2%)
  between operations  16.1 us (2%)
  loops' own time  8.46 us (1%)
    reduce_scatter x1, waiting for transfers between devices, body(): lax.psum_scatter(attn_members[1], 'shard', scatter_dimension=0, tiled=True)  130 us
    unnamed x2, blocking collectives  47 us
    reduce_scatter x1, waiting for transfers between devices, body(): lax.psum_scatter(ffn_members[1], 'shard', scatter_dimension=0, tiled=True)  38.1 us
    psum x1, waiting for transfers between devices, body(): lax.psum(owned_qkv.astype(jnp.bfloat16), 'replica').astype(jnp.float32)  31.1 us
    dot_general x12, matrix products, block_scores(): jnp.einsum('qhd,khd->hqk', query_part, key_part, preferred_element_type=j...  24.6 us
    ppermute x4, waiting for transfers between devices, collect(): earlier.append(lax.ppermute(earlier[-1], axis, up))  24.6 us
    unnamed x103, local copies, waits for them, and re-layouts  23.3 us
    ppermute x3, waiting for transfers between devices, collect(): later.append(lax.ppermute(later[-1], axis, down))  22 us
  transfers between devices with their start and end apart: 16, of which 7 were waited for; matrix products, arithmetic and copies ran while one was open for 52% of the time, Pallas kernels for 0%

profile of v1, /device:TPU:0, one launch (start us, length us, event | category | flops | bytes accessed | tf_op | source)
XLA Modules:
  0.0 749.9 jit_solution(902008537166593724)
XLA Ops:
  16.8 16.5 %collective-permute-done = bf16[96,2304]{1,0:T(8,128)(2,1)S(1)} collective-permute-done((bf16[96,2304]{1,0:T(8,128)(2,1)}, bf16[96,2304]{1,0:T(8,128)(2,1)S(1)}, u32[]{:S(2)}, u32[]{:S(2)}) %collective-permute-start) | collective-permute-done | bytes 442400 | tf_op jit(solution)/shard_map/ppermute | solution.py:22
  40.2 8.0 %collective-permute-done.1 = bf16[96,2304]{1,0:T(8,128)(2,1)S(1)} collective-permute-done((bf16[96,2304]{1,0:T(8,128)(2,1)S(1)}, bf16[96,2304]{1,0:T(8,128)(2,1)S(1)}, u32[]{:S(2)}, u32[]{:S(2)}) %collective-permute-start.1) | collective-permute-done | bytes 442400 | tf_op jit(solution)/shard_map/ppermute | solution.py:22
  52.6 23.9 %all-reduce.13 = (bf16[768]{0:T(1024)(128)(2,1)S(1)}, bf16[768]{0:T(1024)(128)(2,1)S(1)}) all-reduce(bf16[768]{0:T(1024)(128)(2,1)S(1)} %dynamic-update-slice, bf16[768]{0:T(1024)(128)(2,1)S(1)} %dynamic-update-slice.1), channel_id=1, replica_groups=mesh['replica'=4,'shard'=8] {'shard'}, use_global_device_ids=true, to_apply=%add.8 | all-reduce | flops 1536 | bytes 6144
  82.4 17.1 %collective-permute-done.5 = bf16[96,2304]{1,0:T(8,128)(2,1)S(1)} collective-permute-done((bf16[96,2304]{1,0:T(8,128)(2,1)S(1)}, bf16[96,2304]{1,0:T(8,128)(2,1)S(1)}, u32[]{:S(2)}, u32[]{:S(2)}) %collective-permute-start.5) | collective-permute-done | bytes 442400 | tf_op jit(solution)/shard_map/ppermute | solution.py:24
  144.6 5.6 squeeze.70
  174.9 60.9 %while.30 = (s32[]{:T(128)}, bf16[6,512,4,64]{1,3,2,0:T(8,128)(2,1)}, f32[6,4,512]{2,1,0:T(4,128)}, bf16[6,640,4,64]{1,3,2,0:T(8,128)(2,1)}, s32[6]{0:T(128)S(1)...) while((s32[]{:T(128)}, ...), condition=%wide.region_5.6_spmd, body=%wide.region_2.5_spmd.sunk | while | flops 352716416 | bytes 18297728 | solution.py:144
  245.8 10.7 %fusion.112 = f32[1024,2304]{1,0:T(8,128)} fusion(bf16[768,2304]{1,0:T(8,128)(2,1)} %all-gather.7.cloned.1.call-done, f32[1024,768]{0,1:T(8,128)} %copy-done.4, f32[768]{0:T(1024)S(1)} %convert_element_type.164, f32[1024]{0:T(1024)S(1)} %add_rsqrt_fusion, f32[1024]{0:T(1024)S(1)} %broadcast_multiply_fusion.7), kind=kOutput, calls=%fused_computation.205 | convolution fusion | flops 3627024384 | bytes 16133120 | tf_op jit(solution)/shard_map/dot_general | solution.py:220
  256.5 9.2 %fusion.61 = (bf16[1024,1152]{1,0:T(8,128)(2,1)S(1)}, bf16[1024,1152]{1,0:T(8,128)(2,1)S(1)}, bf16[1024,1152]{1,0:T(8,128)(2,1)}) fusion(f32[1024,2304]{1,0:T(8,128)} %fusion.112, bf16[1024,768]{1,0:T(8,128)(2,1)S(1)} %copy-done.21, bf16[1152,768]{1,0:T(8,128)(2,1)} %all-gather.9.cloned.1.call-done), kind=kOutput, calls=%fused_computation.78 | convolution fusion | flops 1830813696 | bytes 19857408 | tf_op jit(solution)/shard_map/td,fd->tf/dot_general | solution.py:240
  276.4 5.5 fusion.115
  294.1 9.3 %fusion.85 = f32[768,2304]{1,0:T(8,128)} fusion(bf16[1024,1152]{1,0:T(8,128)(2,1)} %copy-done.37, bf16[1024,1152]{1,0:T(8,128)(2,1)} %copy-done.36, f32[1024,768]{0,1:T(8,128)S(1)} %copy-done.6, f32[768]{0:T(1024)S(1)} %convert_element_type.164, f32[1024]{0:T(1024)S(1)} %add_rsqrt_fusion, f32[1024]{0:T(1024)S(1)} %broadcast_multiply_fusion.7), kind=kOutput, calls=%fused_computation.125 | convolution fusion | flops 3636461568 | bytes 14953472 | tf_op jit(solution)/shard_map/td,te->de/dot_general | solution.py:245
  303.4 95.7 %while.31 = (s32[]{:T(128)}, f32[6,512,4,64]{1,3,2,0:T(8,128)}, f32[6,640,4,64]{1,3,2,0:T(8,128)}, f32[6,640,4,64]{1,3,2,0:T(8,128)}, bf16[6,640,4,64]{1,3,2,0:T...) while((s32[]{:T(128)}, f32[6,512,4,64]{1,3,2,0:T(8,128)}, ...), condition=%wide.region_12.13_spmd, body=%wide.region_10.12_spmd.sunk | while | flops 860128896 | bytes 44572060 | solution.py:184
  399.1 5.2 copy.70
  418.3 5.2 copy.71
  434.6 5.6 reshape.526
  444.3 5.7 reshape.532
  450.0 6.0 reshape.531
  469.5 6.2 fusion.96
  476.4 9.3 %fusion.76 = (f32[768]{0:T(1024)S(1)}, f32[1024]{0:T(1024)S(1)}, f32[1024]{0:T(1024)S(1)}, f32[1024,768]{0,1:T(8,128)}) fusion(bf16[1024,768]{0,1:T(8,128)(2,1)S(1)} %copy-done.2, f32[1024]{0:T(1024)S(1)} %copy-done.29, f32[1024]{0:T(1024)S(1)} %copy-done.25, f32[768]{0:T(1024)S(1)} %copy-done.27, bf16[768,2304]{1,0:T(8,128)(2,1)} %all-gather.11.cloned.1.call-done, ...), kind=kOutput, calls=%fused_computation.99 | convolution fusion | flops 3630953728 | bytes 12998656 | tf_op jit(solution)/shard_map/te,de->td/dot_general | solution.py:274
  485.7 23.0 %all-reduce.12 = (bf16[768]{0:T(1024)(128)(2,1)S(1)}, bf16[768]{0:T(1024)(128)(2,1)S(1)}) all-reduce(f32[768]{0:T(1024)S(1)} %get-tuple-element.264, f32[768]{0:T(1024)S(1)} %copy-done.30), channel_id=2, replica_groups=mesh['replica'=4,'shard'=8] {'shard'}, use_global_device_ids=true, to_apply=%region_16.17.clone | all-reduce | flops 1536 | bytes 9216
  508.9 6.2 all-reduce.14
  525.1 38.1 %reduce-scatter.9.cloned.1.call-done = f32[96,2304]{1,0:T(8,128)} async-done(((f32[768,2304]{1,0:T(8,128)}), f32[96,2304]{1,0:T(8,128)}) %reduce-scatter.9.cloned.1.call-update) | async-done | bytes 884752 | tf_op jit(solution)/shard_map/reduce_scatter | solution.py:256
  565.2 130.2 %reduce-scatter.5.cloned.1.call-done = f32[96,2304]{1,0:T(8,128)} async-done(((f32[768,2304]{1,0:T(8,128)}), f32[96,2304]{1,0:T(8,128)}) %reduce-scatter.5.cloned.1.call-update) | async-done | bytes 884752 | tf_op jit(solution)/shard_map/reduce_scatter | solution.py:284
  697.4 5.6 add_convert_fusion
  705.6 31.1 %all-reduce.18.cloned.1.call-done = (bf16[96,2304]{1,0:T(8,128)(2,1)}, bf16[96,768]{1,0:T(8,128)(2,1)}, bf16[96,2304]{1,0:T(8,128)(2,1)}, bf16[144,768]{1,0:T(8,128)(2,1)}) async-done(((bf16[96,2304]{1,0:T(8,128)(2,1)}, bf16[96,768]{1,0:T(8,128)(2,1)}, bf16[96,2304]{1,0:T(8,128)(2,1)}, bf16[144,768]{1,0:T(8,128)(2,1)}), (bf16[96,2304]{1,0:T(8,128)(2,1)}, bf16[96,768]{1,0:T(8,128)(2,1)}, ...) | async-done | bytes 1253392 | tf_op jit(solution)/shard_map/psum | solution.py:289
  (351 shorter events, 342.2 us)
Async XLA Ops:
  7.2 43.6 %copy-start.31 = (u32[32]{0:T(128)S(1)}, u32[32]{0:T(128)}, u32[]{:S(2)}) copy-start(u32[32]{0:T(128)} %constant.236) | copy-start | bytes 388
  7.2 44.9 %copy-start.34 = (bf16[96]{0:T(256)(128)(2,1)S(1)}, bf16[96]{0:T(256)(128)(2,1)}, u32[]{:S(2)}) copy-start(bf16[96]{0:T(256)(128)(2,1)} %param.13) | copy-start | bytes 580
  7.2 45.2 %copy-start.35 = (bf16[96]{0:T(256)(128)(2,1)S(1)}, bf16[96]{0:T(256)(128)(2,1)}, u32[]{:S(2)}) copy-start(bf16[96]{0:T(256)(128)(2,1)} %param.16) | copy-start | bytes 580
  7.2 233.2 %all-gather.5.cloned.1.call-start = ((), (), s32[]{:S(2)}) async-start(), calls=%async_computation.4 | async-start | bytes 1327104 | tf_op jit(solution)/shard_map/all_gather | solution.py:198
  7.9 237.9 %all-gather.7.cloned.1.call-start = ((), (), s32[]{:S(2)}) async-start(), calls=%async_computation.5 | async-start | bytes 3981312 | tf_op jit(solution)/shard_map/all_gather | solution.py:202
  8.7 247.8 %all-gather.9.cloned.1.call-start = ((), (), s32[]{:S(2)}) async-start(), calls=%async_computation.6 | async-start | bytes 1990656 | tf_op jit(solution)/shard_map/all_gather | solution.py:203
  9.4 467.0 %all-gather.11.cloned.1.call-start = ((), (), s32[]{:S(2)}) async-start(), calls=%async_computation.7 | async-start | bytes 3981312 | tf_op jit(solution)/shard_map/all_gather | solution.py:230
  9.5 23.8 %collective-permute-start = (bf16[96,2304]{1,0:T(8,128)(2,1)}, bf16[96,2304]{1,0:T(8,128)(2,1)S(1)}, u32[]{:S(2)}, u32[]{:S(2)}) collective-permute-start(bf16[96,2304]{1,0:T(8,128)(2,1)} %param.14), channel_id=1, source_target_pairs={{0,1},{1,2},{2,3},{3,4},{4,5},{5,6},{6,7},{7,0},{8,9},{9,10},{10,1... | collective-permute-start | bytes 1327112 | tf_op jit(solution)/shard_map/ppermute | solution.py:22
  12.5 67.1 %collective-permute-start.4 = (bf16[96,2304]{1,0:T(8,128)(2,1)}, bf16[96,2304]{1,0:T(8,128)(2,1)S(1)}, u32[]{:S(2)}, u32[]{:S(2)}) collective-permute-start(bf16[96,2304]{1,0:T(8,128)(2,1)} %param.14), channel_id=1, source_target_pairs={{0,7},{1,0},{2,1},{3,2},{4,3},{5,4},{6,5},{7,6},{8,15},{9,8},{10,9... | collective-permute-start | bytes 1327112 | tf_op jit(solution)/shard_map/ppermute | solution.py:24
  15.6 505.9 %reduce-scatter.7.cloned.1.call-start = ((), (), s32[]{:S(2)}) async-start(), calls=%async_computation.9 | async-start | bytes 2654208 | tf_op jit(solution)/shard_map/reduce_scatter | solution.py:285
  16.8 104.9 %copy-start.17 = (f32[1024,64]{0,1:T(8,128)}, f32[1024,64]{0,1:T(8,128)S(1)}, u32[]{:S(2)}) copy-start(f32[1024,64]{0,1:T(8,128)S(1)} %get-tuple-element.338) | copy-start | bytes 786436
  16.8 104.9 %copy-start.19 = (f32[1024,64]{0,1:T(8,128)}, f32[1024,64]{0,1:T(8,128)S(1)}, u32[]{:S(2)}) copy-start(f32[1024,64]{0,1:T(8,128)S(1)} %get-tuple-element.339) | copy-start | bytes 786436
  33.3 14.9 %collective-permute-start.1 = (bf16[96,2304]{1,0:T(8,128)(2,1)S(1)}, bf16[96,2304]{1,0:T(8,128)(2,1)S(1)}, u32[]{:S(2)}, u32[]{:S(2)}) collective-permute-start(bf16[96,2304]{1,0:T(8,128)(2,1)S(1)} %collective-permute-done), channel_id=1, source_target_pairs={{0,1},{1,2},{2,3},{3,4},{4,5},{5,6},{6,7},{7,0},{8,9},{9,10},{10,1... | collective-permute-start | bytes 1327112 | tf_op jit(solution)/shard_map/ppermute | solution.py:22
  48.2 33.7 %collective-permute-start.2 = (bf16[96,2304]{1,0:T(8,128)(2,1)S(1)}, bf16[96,2304]{1,0:T(8,128)(2,1)}, u32[]{:S(2)}, u32[]{:S(2)}) collective-permute-start(bf16[96,2304]{1,0:T(8,128)(2,1)S(1)} %collective-permute-done.1), channel_id=1, source_target_pairs={{0,1},{1,2},{2,3},{3,4},{4,5},{5,6},{6,7},{7,0},{8,9},{9,10},{10,1... | collective-permute-start | bytes 1327112 | tf_op jit(solution)/shard_map/ppermute | solution.py:22
  50.7 189.7 %copy-start.1 = (bf16[1024,768]{0,1:T(8,128)(2,1)}, bf16[1024,768]{0,1:T(8,128)(2,1)S(1)}, u32[]{:S(2)}) copy-start(bf16[1024,768]{0,1:T(8,128)(2,1)S(1)} %copy.59) | copy-start | bytes 4718596
  76.5 35.2 %copy-start.26 = (f32[768]{0:T(1024)}, f32[768]{0:T(1024)S(1)}, u32[]{:S(2)}) copy-start(f32[768]{0:T(1024)S(1)} %convert_element_type.157) | copy-start | bytes 9220
  79.6 20.0 %collective-permute-start.5 = (bf16[96,2304]{1,0:T(8,128)(2,1)S(1)}, bf16[96,2304]{1,0:T(8,128)(2,1)S(1)}, u32[]{:S(2)}, u32[]{:S(2)}) collective-permute-start(bf16[96,2304]{1,0:T(8,128)(2,1)S(1)} %collective-permute-done.4), channel_id=1, source_target_pairs={{0,7},{1,0},{2,1},{3,2},{4,3},{5,4},{6,5},{7,6},{8,15},{9,8},{10,9... | collective-permute-start | bytes 1327112 | tf_op jit(solution)/shard_map/ppermute | solution.py:24
  81.9 22.2 %collective-permute-start.3 = (bf16[96,2304]{1,0:T(8,128)(2,1)}, bf16[96,2304]{1,0:T(8,128)(2,1)S(1)}, u32[]{:S(2)}, u32[]{:S(2)}) collective-permute-start(bf16[96,2304]{1,0:T(8,128)(2,1)} %collective-permute-done.2), channel_id=1, source_target_pairs={{0,1},{1,2},{2,3},{3,4},{4,5},{5,6},{6,7},{7,0},{8,9},{9,10},{10,1... | collective-permute-start | bytes 1327112 | tf_op jit(solution)/shard_map/ppermute | solution.py:22
  99.5 10.8 %collective-permute-start.6 = (bf16[96,2304]{1,0:T(8,128)(2,1)S(1)}, bf16[96,2304]{1,0:T(8,128)(2,1)S(1)}, u32[]{:S(2)}, u32[]{:S(2)}) collective-permute-start(bf16[96,2304]{1,0:T(8,128)(2,1)S(1)} %collective-permute-done.5), channel_id=1, source_target_pairs={{0,7},{1,0},{2,1},{3,2},{4,3},{5,4},{6,5},{7,6},{8,15},{9,8},{10,9... | collective-permute-start | bytes 1327112 | tf_op jit(solution)/shard_map/ppermute | solution.py:24
  276.3 247.0 %reduce-scatter.11.cloned.1.call-start = ((), (), s32[]{:S(2)}) async-start(), calls=%async_computation.11 | async-start | bytes 3981312 | tf_op jit(solution)/shard_map/reduce_scatter | solution.py:257
  281.9 281.3 %reduce-scatter.9.cloned.1.call-start = ((), (), s32[]{:S(2)}) async-start(), calls=%async_computation.10 | async-start | bytes 7962624 | tf_op jit(solution)/shard_map/reduce_scatter | solution.py:256
  303.4 392.0 %reduce-scatter.5.cloned.1.call-start = ((), (), s32[]{:S(2)}) async-start(), calls=%async_computation.8 | async-start | bytes 7962624 | tf_op jit(solution)/shard_map/reduce_scatter | solution.py:284
  475.7 261.0 %all-reduce.18.cloned.1.call-start = ((), (), s32[]{:S(2)}) async-start(), calls=%async_computation.12 | async-start | bytes 2506752 | tf_op jit(solution)/shard_map/psum | solution.py:289
  521.6 175.8 %copy-start.7 = (f32[1024,768]{0,1:T(8,128)S(1)}, f32[1024,768]{0,1:T(8,128)}, u32[]{:S(2)}) copy-start(f32[1024,768]{0,1:T(8,128)} %copy-done.4) | copy-start | bytes 9437188
  (31 other events, 200.1 us)
Sparse Core Ops, SparseCore 0:
  10.2 53.4 all-gather.4
  65.9 84.3 all-gather.6
  152.5 44.4 all-gather.8
  199.0 64.1 all-gather.10
  276.5 71.9 reduce-scatter.6
  351.9 78.1 reduce-scatter.10
  433.8 129.3 reduce-scatter.8
  567.3 128.0 reduce-scatter.4
  698.6 38.0 all-reduce.17
